TPU v7x, 32 devices: a whole 2x2x4 slice. The times are simulated.
32 devices in a mesh: dp: 4 (over y, core), wide: 4 (over z), narrow: 2 (over x).
Axes of the slice: x: 2, y: 2, z: 4, core: 2. Of those that a mesh axis runs over, the one named last changes fastest.
Arguments:
- streams: bfloat16 [4, 1024, 2048], P(None, 'dp', ('wide', 'narrow')), may hold values from -6 to 6
- prior: bfloat16 [12, 1024, 2048], P(None, 'dp', ('wide', 'narrow')), may hold values from -6 to 6
- streams_grad: bfloat16 [4, 1024, 2048], P(None, 'dp', ('wide', 'narrow')), may hold values from -6 to 6
- w_qkv: bfloat16 [3, 2048, 2048], P(None, 'wide', 'narrow')
- qkv_bias: bfloat16 [3, 2048], P(None, ('narrow', 'wide')), may hold values from -3 to 3
- w_out: bfloat16 [2048, 2048], P('narrow', 'wide'), may hold values from -1.5 to 1.5
- w_up: bfloat16 [2048, 8192], P('wide', 'narrow')
- up_bias: bfloat16 [8192], P(('narrow', 'wide')), may hold values from -3 to 3
- w_down: bfloat16 [8192, 2048], P('narrow', 'wide'), may hold values from -0.0625 to 0.0625
- branch_bias: bfloat16 [2048], P(('wide', 'narrow')), may hold values from -3 to 3
- norm_gain: bfloat16 [4, 2048], P(None, ('wide', 'narrow')), may hold values from 0.25 to 1.75
- norm_bias: bfloat16 [4, 2048], P(None, ('wide', 'narrow')), may hold values from -2 to 2
- mix_gain: bfloat16 [2048], P(('wide', 'narrow')), may hold values from 0.099609375 to 1.8984375
- mix_in: bfloat16 [2048, 52], P(('wide', 'narrow')), may hold values from -0.125 to 0.125
- mix_out: bfloat16 [52, 52], replicated, may hold values from -0.875 to 0.875
- mix_static: bfloat16 [52], replicated, may hold values from -3 to 3
Outputs:
- streams_out: bfloat16 [4, 1024, 2048], P(None, 'dp', ('wide', 'narrow'))
- streams_in_grad: bfloat16 [4, 1024, 2048], P(None, 'dp', ('wide', 'narrow'))
- prior_grad: bfloat16 [12, 1024, 2048], P(None, 'dp', ('wide', 'narrow'))
- w_qkv_grad: float32 [3, 2048, 2048], P(None, 'wide', 'narrow')
- qkv_bias_grad: float32 [3, 2048], P(None, ('narrow', 'wide'))
- w_out_grad: float32 [2048, 2048], P('narrow', 'wide')
- w_up_grad: float32 [2048, 8192], P('wide', 'narrow')
- up_bias_grad: float32 [8192], P(('narrow', 'wide'))
- w_down_grad: float32 [8192, 2048], P('narrow', 'wide')
- branch_bias_grad: float32 [2048], P(('wide', 'narrow'))
- norm_gain_grad: float32 [4, 2048], P(None, ('wide', 'narrow'))
- norm_bias_grad: float32 [4, 2048], P(None, ('wide', 'narrow'))
- mix_gain_grad: float32 [2048], P(('wide', 'narrow'))
- mix_in_grad: float32 [2048, 52], P(('wide', 'narrow'))
- mix_out_grad: float32 [52, 52], replicated
- mix_static_grad: float32 [52], replicated
All inputs are finite; a program needn't handle non-finite values.
Results may differ from a plain program's by a relative error of at most 0.02.
Values may be sent and summed in bfloat16 or wider, within the bound.
No kernel may reach another device: no remote copies, remote signals or barrier semaphores. Data moves between devices by JAX's collectives and lax.ppermute only.
A program may use at most 192 MiB of HBM per device.

v0:
```python
import math
import jax
import jax.numpy as jnp
from jax import lax
from jax.sharding import PartitionSpec as P

D = 2048
HD = 128
ROT = 32
MIXH = 52
STACK = 13
norm_eps = 1e-05
rms_eps = 1e-06


def model_sum(parts):
    return lax.psum(parts, ("wide", "narrow"))


def gelu_exact(inputs):
    return 0.5 * inputs * (1.0 + lax.erf(inputs * (1.0 / math.sqrt(2.0))))


def gelu_slope(inputs):
    normal_cdf = 0.5 * (1.0 + lax.erf(inputs * (1.0 / math.sqrt(2.0))))
    return normal_cdf + inputs * jnp.exp(-0.5 * inputs * inputs) * (1.0 / math.sqrt(2.0 * math.pi))


def rotate(heads_in, cosine, sine_table, direction):
    half = ROT // 2
    first = heads_in[..., :half]
    second = heads_in[..., half:ROT]
    rest_part = heads_in[..., ROT:]
    cos_b = cosine[:, None, :]
    sin_b = direction * sine_table[:, None, :]
    return jnp.concatenate(
        [first * cos_b - second * sin_b, second * cos_b + first * sin_b, rest_part], axis=-1
    )


def masked_scores(query_rows, key_heads, row_start, row_block, length, scale):
    scores = (
        jnp.einsum("qhd,khd->hqk", query_rows, key_heads, preferred_element_type=jnp.float32)
        * scale
    )
    row_ids = row_start + lax.broadcasted_iota(jnp.int32, (row_block, length), 0)
    col_ids = lax.broadcasted_iota(jnp.int32, (row_block, length), 1)
    return jnp.where((col_ids <= row_ids)[None], scores, -1e30)


def attend_rows(queries, key_heads, value_heads, scale):
    length = queries.shape[0]
    row_block = min(512, length)

    def one_block(block_index):
        row_start = block_index * row_block
        scores = masked_scores(queries, key_heads, row_start, row_block, length, scale)
        row_top = jnp.max(scores, axis=2, keepdims=True)
        log_total = row_top + jnp.log(jnp.sum(jnp.exp(scores - row_top), axis=2, keepdims=True))
        attn_probs = jnp.exp(scores - log_total).astype(jnp.bfloat16)
        output = jnp.einsum(
            "hqk,khd->qhd", attn_probs, value_heads, preferred_element_type=jnp.float32
        )
        return (output, log_total[:, :, 0])

    outputs, totals = lax.map(one_block, jnp.arange(length // row_block, dtype=jnp.int32))
    return (outputs.reshape(queries.shape), totals)


def attend_back(queries, key_heads, value_heads, out_grad, totals, scale):
    length = queries.shape[0]
    row_block = min(512, length)

    def one_block(carry, block_index):
        key_grad, value_grad = carry
        row_start = block_index * row_block
        log_total = lax.dynamic_index_in_dim(totals, block_index, 0, keepdims=False)
        scores = masked_scores(queries, key_heads, row_start, row_block, length, scale)
        attn_probs = jnp.exp(scores - log_total[:, :, None])
        probs_low = attn_probs.astype(jnp.bfloat16)
        value_grad = value_grad + jnp.einsum(
            "hqk,qhd->khd", probs_low, out_grad, preferred_element_type=jnp.float32
        )
        prob_grad = jnp.einsum(
            "qhd,khd->hqk", out_grad, value_heads, preferred_element_type=jnp.float32
        )
        row_dot = jnp.sum(attn_probs * prob_grad, axis=2, keepdims=True)
        score_grad = (attn_probs * (prob_grad - row_dot)).astype(jnp.bfloat16)
        query_grad = (
            jnp.einsum("hqk,khd->qhd", score_grad, key_heads, preferred_element_type=jnp.float32)
            * scale
        )
        key_grad = (
            key_grad
            + jnp.einsum("hqk,qhd->khd", score_grad, queries, preferred_element_type=jnp.float32)
            * scale
        )
        return ((key_grad, value_grad), query_grad)

    zero_heads = jnp.zeros(queries.shape, jnp.float32)
    (key_grad, value_grad), query_blocks = lax.scan(
        one_block, (zero_heads, zero_heads), jnp.arange(length // row_block, dtype=jnp.int32)
    )
    return (query_blocks.reshape(queries.shape), key_grad, value_grad)


def contract_rows(left, right):
    return lax.dot_general(
        left, right, (((0,), (0,)), ((), ())), preferred_element_type=jnp.float32
    )


def contract_cols(left, right):
    return lax.dot_general(
        left, right, (((1,), (1,)), ((), ())), preferred_element_type=jnp.float32
    )


def per_device(
    streams,
    prior,
    streams_grad,
    w_qkv,
    qkv_bias,
    w_out,
    w_up,
    up_bias,
    w_down,
    branch_bias,
    norm_gain,
    norm_bias,
    mix_gain,
    mix_in,
    mix_out,
    mix_static,
):
    high = lax.Precision.HIGHEST
    length = streams.shape[1]
    local_cols = streams.shape[2]
    heads_here = local_cols // HD
    scale = 1.0 / math.sqrt(HD)
    inputs = streams.astype(jnp.float32)
    row_total, row_squares = model_sum((jnp.sum(inputs, axis=2), jnp.sum(inputs * inputs, axis=2)))
    row_mean = row_total / D
    inv_std = lax.rsqrt(row_squares / D - row_mean * row_mean + norm_eps)
    centred = (inputs - row_mean[:, :, None]) * inv_std[:, :, None]
    norm_scale = norm_gain.astype(jnp.float32)[:, None, :]
    normed = (centred * norm_scale + norm_bias.astype(jnp.float32)[:, None, :]).astype(jnp.bfloat16)
    near_cols = lax.all_gather(normed, "narrow", axis=2, tiled=True)
    qkv_part = jnp.einsum("std,sdf->stf", near_cols[:3], w_qkv, preferred_element_type=jnp.float32)
    up_part = jnp.dot(near_cols[3], w_up, preferred_element_type=jnp.float32)
    qkv_pre, up_summed = (
        lax.psum_scatter(qkv_part, "wide", scatter_dimension=2, tiled=True),
        lax.psum_scatter(up_part[None], "wide", scatter_dimension=2, tiled=True),
    )
    up_pre = up_summed[0]
    qkv_pre = qkv_pre + qkv_bias.astype(jnp.float32)[:, None, :]
    up_pre = up_pre + up_bias.astype(jnp.float32)[None, :]
    positions = lax.iota(jnp.float32, length)
    freqs = jnp.exp(lax.iota(jnp.float32, ROT // 2) * (-2.0 * math.log(10000.0) / ROT))
    angles = positions[:, None] * freqs[None, :]
    cosine = jnp.cos(angles)
    sine_table = jnp.sin(angles)
    head_view = qkv_pre.reshape(3, length, heads_here, HD)
    queries = rotate(head_view[0], cosine, sine_table, 1.0).astype(jnp.bfloat16)
    key_heads = rotate(head_view[1], cosine, sine_table, 1.0).astype(jnp.bfloat16)
    value_heads = head_view[2].astype(jnp.bfloat16)
    attn_heads, totals = attend_rows(queries, key_heads, value_heads, scale)
    attn_low = attn_heads.reshape(length, local_cols).astype(jnp.bfloat16)
    hidden = gelu_exact(up_pre).astype(jnp.bfloat16)
    attn_wide, hidden_wide = (
        lax.all_gather(attn_low, "wide", axis=1, tiled=True),
        lax.all_gather(hidden, "wide", axis=1, tiled=True),
    )
    branch_part = jnp.dot(attn_wide, w_out, preferred_element_type=jnp.float32) + jnp.dot(
        hidden_wide, w_down, preferred_element_type=jnp.float32
    )
    branch = (
        lax.psum_scatter(branch_part, "narrow", scatter_dimension=1, tiled=True)
        + branch_bias.astype(jnp.float32)[None, :]
    )
    layer_out = inputs[3] + branch
    mix_scale = mix_gain.astype(jnp.float32)
    scaled = layer_out * mix_scale[None, :]
    mix_weight = mix_in.astype(jnp.float32)
    mix_back = mix_out.astype(jnp.float32)
    energy, logit_sum = model_sum(
        (jnp.sum(layer_out * layer_out, axis=1), jnp.dot(scaled, mix_weight, precision=high))
    )
    rms = lax.rsqrt(energy / D + rms_eps)
    logits = logit_sum * rms[:, None]
    mix_hidden = gelu_exact(logits)
    weights = (
        jnp.dot(mix_hidden, mix_back, precision=high) + mix_static.astype(jnp.float32)[None, :]
    )
    coef = weights.reshape(length, 4, STACK)
    prior_vals = prior.astype(jnp.float32)
    mixed = jnp.einsum("tsj,jtl->stl", coef[:, :, : STACK - 1], prior_vals, precision=high)
    streams_out = (
        mixed + jnp.transpose(coef[:, :, STACK - 1])[:, :, None] * layer_out[None]
    ).astype(jnp.bfloat16)
    grad_out = streams_grad.astype(jnp.float32)
    prior_part = jnp.einsum("stl,jtl->tsj", grad_out, prior_vals, precision=high)
    layer_part = jnp.einsum("stl,tl->ts", grad_out, layer_out, precision=high)
    coef_part = jnp.concatenate([prior_part, layer_part[:, :, None]], axis=2).reshape(length, MIXH)
    (coef_grad,) = model_sum((coef_part,))
    prior_grad = jnp.einsum(
        "tsj,stl->jtl", coef[:, :, : STACK - 1], grad_out, precision=high
    ).astype(jnp.bfloat16)
    layer_grad = jnp.einsum("ts,stl->tl", coef[:, :, STACK - 1], grad_out, precision=high)
    static_grad = jnp.sum(coef_grad, axis=0)
    mix_out_grad = jnp.dot(mix_hidden.T, coef_grad, precision=high)
    logit_grad = jnp.dot(coef_grad, mix_back.T, precision=high) * gelu_slope(logits)
    sum_grad = logit_grad * rms[:, None]
    rms_grad = jnp.sum(logit_grad * logit_sum, axis=1)
    energy_grad = -0.5 * rms_grad * rms * rms * rms / D
    mix_in_grad = jnp.dot(scaled.T, sum_grad, precision=high)
    scaled_grad = jnp.dot(sum_grad, mix_weight.T, precision=high)
    mix_gain_grad = jnp.sum(scaled_grad * layer_out, axis=0)
    layer_grad = (
        layer_grad + scaled_grad * mix_scale[None, :] + 2.0 * energy_grad[:, None] * layer_out
    )
    branch_grad = layer_grad.astype(jnp.bfloat16)
    branch_bias_grad = jnp.sum(branch_grad.astype(jnp.float32), axis=0)
    branch_near = lax.all_gather(branch_grad, "narrow", axis=1, tiled=True)
    attn_grad, hidden_grad = (
        lax.psum_scatter(
            contract_cols(branch_near, w_out), "wide", scatter_dimension=1, tiled=True
        ),
        lax.psum_scatter(
            contract_cols(branch_near, w_down), "wide", scatter_dimension=1, tiled=True
        ),
    )
    out_weight_grad = contract_rows(attn_wide, branch_near)
    down_weight_grad = contract_rows(hidden_wide, branch_near)
    attn_low_grad = attn_grad.astype(jnp.bfloat16).reshape(length, heads_here, HD)
    up_grad = (hidden_grad * gelu_slope(up_pre)).astype(jnp.bfloat16)
    up_bias_grad = jnp.sum(up_grad.astype(jnp.float32), axis=0)
    query_grad, key_grad, value_grad = attend_back(
        queries, key_heads, value_heads, attn_low_grad, totals, scale
    )
    query_pre = rotate(query_grad, cosine, sine_table, -1.0).reshape(length, local_cols)
    key_pre = rotate(key_grad, cosine, sine_table, -1.0).reshape(length, local_cols)
    projected_grad = jnp.stack([query_pre, key_pre, value_grad.reshape(length, local_cols)]).astype(
        jnp.bfloat16
    )
    qkv_bias_grad = jnp.sum(projected_grad.astype(jnp.float32), axis=1)
    far_qkv, far_up = (
        lax.all_gather(projected_grad, "wide", axis=2, tiled=True),
        lax.all_gather(up_grad[None], "wide", axis=2, tiled=True),
    )
    qkv_weight_grad = jnp.einsum(
        "std,stf->sdf", near_cols[:3], far_qkv, preferred_element_type=jnp.float32
    )
    up_weight_grad = contract_rows(near_cols[3], far_up[0])
    normed_part = jnp.concatenate(
        [
            jnp.einsum("stf,sdf->std", far_qkv, w_qkv, preferred_element_type=jnp.float32),
            contract_cols(far_up[0], w_up)[None],
        ],
        axis=0,
    )
    normed_grad = lax.psum_scatter(normed_part, "narrow", scatter_dimension=2, tiled=True)
    gain_grad = jnp.sum(normed_grad * centred, axis=1)
    shift_grad = jnp.sum(normed_grad, axis=1)
    centred_grad = normed_grad * norm_scale
    grad_total, grad_cross = model_sum(
        (jnp.sum(centred_grad, axis=2), jnp.sum(centred_grad * centred, axis=2))
    )
    input_grad = inv_std[:, :, None] * (
        centred_grad - (grad_total / D)[:, :, None] - centred * (grad_cross / D)[:, :, None]
    )
    input_grad = input_grad.at[3].add(layer_grad)
    streams_in_grad = input_grad.astype(jnp.bfloat16)
    summed = lax.psum(
        (
            qkv_weight_grad,
            qkv_bias_grad,
            out_weight_grad,
            up_weight_grad,
            up_bias_grad,
            down_weight_grad,
            branch_bias_grad,
            gain_grad,
            shift_grad,
            mix_gain_grad,
            mix_in_grad,
            mix_out_grad,
            static_grad,
        ),
        "dp",
    )
    return (
        streams_out,
        streams_in_grad,
        prior_grad,
        summed[0],
        summed[1],
        summed[2],
        summed[3],
        summed[4],
        summed[5],
        summed[6],
        summed[7],
        summed[8],
        summed[9],
        summed[10],
        summed[11],
        summed[12],
    )


def solution(mesh):
    return jax.shard_map(
        per_device,
        mesh=mesh,
        in_specs=(
            P(None, "dp", ("wide", "narrow")),
            P(None, "dp", ("wide", "narrow")),
            P(None, "dp", ("wide", "narrow")),
            P(None, "wide", "narrow"),
            P(None, ("narrow", "wide")),
            P("narrow", "wide"),
            P("wide", "narrow"),
            P(("narrow", "wide")),
            P("narrow", "wide"),
            P(("wide", "narrow")),
            P(None, ("wide", "narrow")),
            P(None, ("wide", "narrow")),
            P(("wide", "narrow")),
            P(("wide", "narrow"), None),
            P(),
            P(),
        ),
        out_specs=(
            P(None, "dp", ("wide", "narrow")),
            P(None, "dp", ("wide", "narrow")),
            P(None, "dp", ("wide", "narrow")),
            P(None, "wide", "narrow"),
            P(None, ("narrow", "wide")),
            P("narrow", "wide"),
            P("wide", "narrow"),
            P(("narrow", "wide")),
            P("narrow", "wide"),
            P(("wide", "narrow")),
            P(None, ("wide", "narrow")),
            P(None, ("wide", "narrow")),
            P(("wide", "narrow")),
            P(("wide", "narrow"), None),
            P(),
            P(),
        ),
        check_vma=False,
    )
```

profile of v0, /device:TPU:0, one launch (start us, length us, event | category | flops | bytes accessed | tf_op | source)
XLA Modules:
  0.0 1101.8 jit_solution(11456983785825005663)
XLA Ops:
  10.2 23.3 %all-reduce.2 = (f32[4,256]{1,0:T(4,128)S(1)}, f32[4,256]{1,0:T(4,128)S(1)}) all-reduce(f32[4,256]{1,0:T(4,128)S(1)} %get-tuple-element.142, f32[4,256]{1,0:T(4,128)S(1)} %get-tuple-element.141), channel_id=1, replica_groups=mesh['dp'=4,'wide'=4,'narrow'=2] {'wide','narrow'}, use_global_device_ids=true, to_apply=%region_3.0 | all-reduce | flops 2048 | bytes 16384 | tf_op jit(solution)/shard_map/psum | solution.py:17
  33.5 2.2 add_convert_fusion
  35.8 18.7 %all-gather.6.cloned.1.call-done = bf16[4,256,512]{2,1,0:T(8,128)(2,1)} async-done(((bf16[4,256,256]{2,1,0:T(8,128)(2,1)}), bf16[4,256,512]{2,1,0:T(8,128)(2,1)}) %all-gather.6.cloned.1.call-update) | async-done | bytes 1048592 | tf_op jit(solution)/shard_map/all_gather | solution.py:149
  54.4 5.6 convolution_bitcast_fusion
  60.1 3.8 fusion.72
  64.6 72.4 %reduce-scatter.9.cloned.1.call-done = f32[1,256,1024]{2,1,0:T(8,128)} async-done(((f32[1,256,4096]{2,1,0:T(8,128)}), f32[1,256,1024]{2,1,0:T(8,128)}) %reduce-scatter.9.cloned.1.call-update) | async-done | bytes 1048592 | tf_op jit(solution)/shard_map/reduce_scatter | solution.py:154
  136.9 2.2 multiply_convert_fusion
  141.1 59.6 %reduce-scatter.7.cloned.1.call-done = f32[3,256,256]{2,1,0:T(8,128)} async-done(((f32[3,256,1024]{2,1,0:T(8,128)}), f32[3,256,256]{2,1,0:T(8,128)}) %reduce-scatter.7.cloned.1.call-update) | async-done | bytes 786448 | tf_op jit(solution)/shard_map/reduce_scatter | solution.py:153
  204.5 1.8 squeeze.37
  210.6 1.7 fusion.63
  214.0 22.1 %all_gather.19 = bf16[256,1024]{0,1:T(8,128)(2,1)} all-gather(bf16[256,256]{0,1:T(8,128)(2,1)S(1)} %bitcast.112), channel_id=1, replica_groups=mesh['dp'=4,'wide'=4,'narrow'=2] {'wide'}, dimensions={1}, use_global_device_ids=true | all-gather | bytes 655360 | tf_op jit(solution)/shard_map/all_gather | solution.py:172
  236.2 20.9 %all-gather.8.cloned.1.call-done = bf16[256,4096]{1,0:T(8,128)(2,1)} async-done(((bf16[256,1024]{1,0:T(8,128)(2,1)}), bf16[256,4096]{1,0:T(8,128)(2,1)}) %all-gather.8.cloned.1.call-update) | async-done | bytes 2097168 | tf_op jit(solution)/shard_map/all_gather | solution.py:173
  257.1 4.2 fusion.66
  262.6 2.1 convert_element_type.90
  265.9 3.7 fusion
  269.6 6.5 reduce-scatter.11.cloned.1.call-done
  276.1 1.8 multiply_reduce_fusion.6
  277.9 2.6 convolution_bitcast_fusion.2
  281.7 1.9 copy.142
  288.1 68.3 %all-reduce.9.cloned.1.call-done = (f32[256,52]{0,1:T(8,128)}, f32[256]{0:T(256)}, f32[256,52]{0,1:T(8,128)}) async-done(((f32[256,52]{0,1:T(8,128)}, f32[256]{0:T(256)}, f32[256,52]{0,1:T(8,128)}), (f32[256,52]{0,1:T(8,128)}, f32[256]{0:T(256)}, f32[256,52]{0,1:T(8,128)})) %all-reduce.9.cloned.1.call-update) | async-done | bytes 107536 | tf_op jit(solution)/shard_map/psum | solution.py:17
  359.9 1.7 convolution_add_fusion.1
  365.9 2.4 fusion.34
  368.3 2.4 convert_reduce_fusion.3
  370.7 5.6 all_gather.21
  377.9 5.5 fusion.69
  383.4 21.7 %reduce-scatter.13.cloned.1.call-done = f32[256,256]{1,0:T(8,128)} async-done(((f32[256,1024]{1,0:T(8,128)}), f32[256,256]{1,0:T(8,128)}) %reduce-scatter.13.cloned.1.call-update) | async-done | bytes 262160 | tf_op jit(solution)/shard_map/reduce_scatter | solution.py:227
  416.2 1.8 pad_maximum_fusion.6
  419.8 2.0 convolution_convert_fusion
  422.9 2.4 convert_reduce_fusion.1
  425.3 58.1 %reduce-scatter.15.cloned.1.call-done = f32[256,1024]{1,0:T(8,128)} async-done(((f32[256,4096]{1,0:T(8,128)}), f32[256,1024]{1,0:T(8,128)}) %reduce-scatter.15.cloned.1.call-update) | async-done | bytes 1048592 | tf_op jit(solution)/shard_map/reduce_scatter | solution.py:230
  483.5 3.4 convert_reduce_fusion
  487.0 36.9 %all-gather.10.cloned.1.call-done = bf16[3,256,1024]{2,1,0:T(8,128)(2,1)} async-done(((bf16[3,256,256]{2,1,0:T(8,128)(2,1)}), bf16[3,256,1024]{2,1,0:T(8,128)(2,1)}) %all-gather.10.cloned.1.call-update) | async-done | bytes 1572880 | tf_op jit(solution)/shard_map/all_gather | solution.py:249
  523.9 3.6 fusion.68
  527.5 42.7 %all-gather.12.cloned.1.call-done = bf16[256,4096]{1,0:T(8,128)(2,1)} async-done(((bf16[256,1024]{1,0:T(8,128)(2,1)}), bf16[256,4096]{1,0:T(8,128)(2,1)}) %all-gather.12.cloned.1.call-update) | async-done | bytes 2097168 | tf_op jit(solution)/shard_map/all_gather | solution.py:250
  570.2 4.1 convolution_bitcast_fusion.1
  579.0 1.8 fusion.70
  580.9 4.7 fusion.71
  585.6 3.8 fusion.73
  589.4 17.2 %reduce-scatter.17.cloned.1.call-done = f32[4,256,256]{2,1,0:T(8,128)} async-done(((f32[4,256,512]{2,1,0:T(8,128)}), f32[4,256,256]{2,1,0:T(8,128)}) %reduce-scatter.17.cloned.1.call-update) | async-done | bytes 1048592 | tf_op jit(solution)/shard_map/reduce_scatter | solution.py:263
  606.6 2.6 multiply_reduce_fusion
  609.3 5.6 fusion.31
  616.8 3.3 convert_bitcast_fusion
  621.9 3.7 fusion.10
  626.4 20.7 %all-reduce = (f32[4,256]{1,0:T(4,128)S(1)}, f32[4,256]{1,0:T(4,128)S(1)}) all-reduce(f32[4,256]{1,0:T(4,128)S(1)} %get-tuple-element.138, f32[4,256]{1,0:T(4,128)S(1)} %get-tuple-element.139), channel_id=1, replica_groups=mesh['dp'=4,'wide'=4,'narrow'=2] {'wide','narrow'}, use_global_device_ids=true, to_apply=%region_21.22 | all-reduce | flops 2048 | bytes 16384 | tf_op jit(solution)/shard_map/psum | solution.py:17
  648.8 423.5 %all-reduce.13.cloned.1.call-done = (f32[3,512,1024]{2,1,0:T(8,128)}, f32[1024,512]{1,0:T(8,128)}, f32[512,4096]{1,0:T(8,128)}, f32[4096,512]{1,0:T(8,128)}) async-done(((f32[3,512,1024]{2,1,0:T(8,128)}, f32[1024,512]{1,0:T(8,128)}, f32[512,4096]{1,0:T(8,128)}, f32[4096,512]{1,0:T(8,128)}), (f32[3,512,1024]{2,1,0:T(8,128)}, f32[1024,512]{1,0:T(8,128)}, f32[512,4096]{1,0:T(8,128)}, ...) | async-done | bytes 25165840 | tf_op jit(solution)/shard_map/psum | solution.py:275
  1072.3 7.1 copy.244
  1081.3 4.3 copy.247
  1087.3 3.9 copy.249
  (224 shorter events, 65.3 us)
Async XLA Ops:
  7.2 52.9 %copy-start = (bf16[3,512,1024]{2,1,0:T(8,128)(2,1)S(1)}, bf16[3,512,1024]{2,1,0:T(8,128)(2,1)}, u32[]{:S(2)}) copy-start(bf16[3,512,1024]{2,1,0:T(8,128)(2,1)} %param.21) | copy-start | bytes 9437188
  7.2 47.2 %all-gather.6.cloned.1.call-start = ((), (), s32[]{:S(2)}) async-start(), calls=%async_computation.6 | async-start | bytes 1572864 | tf_op jit(solution)/shard_map/all_gather | solution.py:149
  35.7 101.2 %reduce-scatter.9.cloned.1.call-start = ((), (), s32[]{:S(2)}) async-start(), calls=%async_computation.8 | async-start | bytes 5242880 | tf_op jit(solution)/shard_map/reduce_scatter | solution.py:154
  60.0 140.7 %reduce-scatter.7.cloned.1.call-start = ((), (), s32[]{:S(2)}) async-start(), calls=%async_computation.7 | async-start | bytes 3932160 | tf_op jit(solution)/shard_map/reduce_scatter | solution.py:153
  63.9 75.4 %copy-start.52 = (bf16[3,256]{1,0:T(4,128)(2,1)S(1)}, bf16[3,256]{1,0:T(4,128)(2,1)}, u32[]{:S(2)}) copy-start(bf16[3,256]{1,0:T(4,128)(2,1)} %param.22) | copy-start | bytes 4612
  63.9 193.2 %all-gather.8.cloned.1.call-start = ((), (), s32[]{:S(2)}) async-start(), calls=%async_computation.9 | async-start | bytes 2621440 | tf_op jit(solution)/shard_map/all_gather | solution.py:173
  64.6 138.0 %copy-start.41 = (f32[1024]{0:T(1024)}, f32[1024]{0:T(1024)S(1)}, u32[]{:S(2)}) copy-start(f32[1024]{0:T(1024)S(1)} %convert_element_type.100) | copy-start | bytes 12292
  139.2 136.9 %reduce-scatter.11.cloned.1.call-start = ((), (), s32[]{:S(2)}) async-start(), calls=%async_computation.10 | async-start | bytes 786432 | tf_op jit(solution)/shard_map/reduce_scatter | solution.py:179
  257.1 4.2 copy-start.6
  257.1 4.2 copy-start.11
  261.3 3.5 copy-start.55
  261.3 4.0 copy-start.56
  262.6 93.8 %all-reduce.9.cloned.1.call-start = ((), (), s32[]{:S(2)}) async-start(), calls=%async_computation.16 | async-start | bytes 231424 | tf_op jit(solution)/shard_map/psum | solution.py:17
  276.1 4.4 copy-start.33
  277.9 90.4 %copy-start.9 = (f32[256,256]{1,0:T(8,128)}, f32[256,256]{1,0:T(8,128)S(1)}, u32[]{:S(2)}) copy-start(f32[256,256]{1,0:T(8,128)S(1)} %get-tuple-element.171) | copy-start | bytes 786436
  286.7 118.5 %reduce-scatter.13.cloned.1.call-start = ((), (), s32[]{:S(2)}) async-start(), calls=%async_computation.11 | async-start | bytes 1310720 | tf_op jit(solution)/shard_map/reduce_scatter | solution.py:227
  365.9 10.5 copy-start.12
  377.8 105.6 %reduce-scatter.15.cloned.1.call-start = ((), (), s32[]{:S(2)}) async-start(), calls=%async_computation.13 | async-start | bytes 5242880 | tf_op jit(solution)/shard_map/reduce_scatter | solution.py:230
  383.4 140.5 %all-gather.10.cloned.1.call-start = ((), (), s32[]{:S(2)}) async-start(), calls=%async_computation.12 | async-start | bytes 1966080 | tf_op jit(solution)/shard_map/all_gather | solution.py:249
  408.4 3.2 copy-start.18
  408.4 3.2 copy-start.20
  408.5 3.2 copy-start.27
  425.3 144.9 %all-gather.12.cloned.1.call-start = ((), (), s32[]{:S(2)}) async-start(), calls=%async_computation.15 | async-start | bytes 2621440 | tf_op jit(solution)/shard_map/all_gather | solution.py:250
  486.9 119.6 %reduce-scatter.17.cloned.1.call-start = ((), (), s32[]{:S(2)}) async-start(), calls=%async_computation.14 | async-start | bytes 3145728 | tf_op jit(solution)/shard_map/reduce_scatter | solution.py:263
  527.5 46.8 %copy-start.5 = (f32[3,256,512]{2,1,0:T(8,128)S(1)}, f32[3,256,512]{2,1,0:T(8,128)}, u32[]{:S(2)}) copy-start(f32[3,256,512]{2,1,0:T(8,128)} %fusion.68) | copy-start | bytes 4718596
  575.9 5.0 copy-start.13
  575.9 72.9 %all-reduce.11.cloned.1.call-start = ((), (), s32[]{:S(2)}) async-start(), calls=%async_computation.17 | async-start | bytes 209920 | tf_op jit(solution)/shard_map/psum | solution.py:275
  580.9 4.7 copy-start.16
  580.9 4.7 copy-start.34
  585.6 21.0 %copy-start.3 = (bf16[4,256,256]{2,1,0:T(8,128)(2,1)S(1)}, bf16[4,256,256]{2,1,0:T(8,128)(2,1)}, u32[]{:S(2)}) copy-start(bf16[4,256,256]{2,1,0:T(8,128)(2,1)} %param.18) | copy-start | bytes 1572868
  585.6 23.7 %copy-start.15 = (bf16[256,4096]{1,0:T(8,128)(2,1)S(1)}, bf16[256,4096]{1,0:T(8,128)(2,1)}, u32[]{:S(2)}) copy-start(bf16[256,4096]{1,0:T(8,128)(2,1)} %all-gather.12.cloned.1.call-done) | copy-start | bytes 6291460
  609.2 463.0 %all-reduce.13.cloned.1.call-start = ((), (), s32[]{:S(2)}) async-start(), calls=%async_computation.18 | async-start | bytes 50331648 | tf_op jit(solution)/shard_map/psum | solution.py:275
  621.9 25.3 %copy-start.8 = (f32[4,256,256]{2,1,0:T(8,128)S(1)}, f32[4,256,256]{2,1,0:T(8,128)}, u32[]{:S(2)}) copy-start(f32[4,256,256]{2,1,0:T(8,128)} %reduce-scatter.17.cloned.1.call-done) | copy-start | bytes 3145732
  625.5 22.3 %copy-start.30 = (f32[256,256]{1,0:T(8,128)S(1)}, f32[256,256]{1,0:T(8,128)}, u32[]{:S(2)}) copy-start(f32[256,256]{1,0:T(8,128)} %get-tuple-element.165) | copy-start | bytes 786436
  1072.2 7.1 copy-start.50
  1072.3 7.7 copy-start.14
  1072.3 9.0 copy-start.4
  1079.9 6.2 slice-start
  1081.2 4.3 copy-start.49
  1081.2 6.0 slice-start.1
  1087.2 4.0 copy-start.54
  1087.2 4.5 copy-start.48
  1087.2 5.1 copy-start.47
  1087.2 5.7 copy-start.53
  1087.3 6.3 copy-start.40
  1087.3 6.9 copy-start.43
  1087.3 7.5 copy-start.57
  1087.3 8.0 copy-start.1
  (25 other events, 45.7 us)
Sparse Core Ops, SparseCore 0:
  35.8 18.5 all-gather.5
  60.1 76.7 reduce-scatter.8
  139.9 60.7 reduce-scatter.6
  202.8 54.2 all-gather.7
  262.7 13.3 reduce-scatter.10
  286.8 69.5 all-reduce.8
  377.9 27.1 reduce-scatter.12
  408.0 75.4 reduce-scatter.14
  485.7 38.1 all-gather.9
  526.0 44.1 all-gather.11
  576.0 30.5 reduce-scatter.16
  610.6 30.8 all-reduce.10
  645.6 426.6 all-reduce.12
where the time goes:
time: 1100 us
  waiting for transfers between devices  847 us (77%)
  matrix products  75 us (7%)
  blocking collectives  71.8 us (7%)
  local copies, waits for them, and re-layouts  54.5 us (5%)
  other arithmetic  38.3 us (3%)
  between operations  14.6 us (1%)
    psum x2, waiting for transfers between devices, per_device(): lax.psum((qkv_weight_grad, qkv_bias_grad, out_weight_grad, up_weight_grad...  423 us
    reduce_scatter x1, waiting for transfers between devices, per_device(): lax.psum_scatter(up_part[None], 'wide', scatter_dimension=2, tiled=True)  72.4 us
    psum x1, waiting for transfers between devices, model_sum(): return lax.psum(parts, ('wide', 'narrow'))  68.3 us
    reduce_scatter x1, waiting for transfers between devices, per_device(): lax.psum_scatter(qkv_part, 'wide', scatter_dimension=2, tiled=True)  59.6 us
    reduce_scatter x1, waiting for transfers between devices, per_device(): lax.psum_scatter(contract_cols(branch_near, w_down), 'wide', scatter_dime...  58.1 us
    psum x2, blocking collectives, model_sum(): return lax.psum(parts, ('wide', 'narrow'))  44 us
    all_gather x1, waiting for transfers between devices, per_device(): lax.all_gather(up_grad[None], 'wide', axis=2, tiled=True)  42.7 us
    all_gather x1, waiting for transfers between devices, per_device(): lax.all_gather(projected_grad, 'wide', axis=2, tiled=True)  36.9 us
  transfers between devices with their start and end apart: 13, of which 12 were waited for; matrix products, arithmetic and copies ran while one was open for 8% of the time, Pallas kernels for 0%

commit v1 on v0

--- a/solution.py
+++ b/solution.py
@@ -11,6 +11,27 @@
 STACK = 13
 norm_eps = 1e-05
 rms_eps = 1e-06
+
+
+def gather_around(x, axis, dim):
+    size, index, width = (lax.axis_size(axis), lax.axis_index(axis), x.shape[dim])
+    ahead = [(i, (i + 1) % size) for i in range(size)]
+    left = [(i, (i - 1) % size) for i in range(size)]
+    filled = jnp.zeros((*x.shape[:dim], size * width, *x.shape[dim + 1 :]), x.dtype)
+    filled = lax.dynamic_update_slice_in_dim(filled, x, index * width, axis=dim)
+    from_left = from_right = x
+    middle = size // 2
+    for step in range(1, middle + 1):
+        from_left = lax.ppermute(from_left, axis, ahead)
+        filled = lax.dynamic_update_slice_in_dim(
+            filled, from_left, (index - step) % size * width, axis=dim
+        )
+        if step < size - middle:
+            from_right = lax.ppermute(from_right, axis, left)
+            filled = lax.dynamic_update_slice_in_dim(
+                filled, from_right, (index + step) % size * width, axis=dim
+            )
+    return filled
 
 
 def model_sum(parts):
@@ -246,7 +267,7 @@
     )
     qkv_bias_grad = jnp.sum(projected_grad.astype(jnp.float32), axis=1)
     far_qkv, far_up = (
-        lax.all_gather(projected_grad, "wide", axis=2, tiled=True),
+        gather_around(projected_grad, "wide", 2),
         lax.all_gather(up_grad[None], "wide", axis=2, tiled=True),
     )
     qkv_weight_grad = jnp.einsum(

time: 1100 us -> 1100 us (level)
  waiting for transfers between devices: 847 us -> 813 us
  starting transfers between devices: 0.94 us -> 17.1 us
  local copies, waits for them, and re-layouts: 54.5 us -> 68.7 us
    all_gather x1, waiting for transfers between devices: 42.7 us -> 0.01 us  [per_device(): lax.all_gather(up_grad[None], 'wide', axis=2, tiled=True)]
    all_gather x1 -> x0, waiting for transfers between devices: 36.9 us -> none  [per_device(): lax.all_gather(projected_grad, 'wide', axis=2, tiled=True)]
    ppermute x0 -> x3, waiting for transfers between devices: none -> 26.2 us  [the longest x2 26.2 us: gather_around(): from_left = lax.ppermute(from_left, axis, ahead)]
    ppermute x0 -> x3, starting transfers between devices: none -> 16.2 us  [the longest x2 12.4 us: gather_around(): from_left = lax.ppermute(from_left, axis, ahead)]
    reduce_scatter x1, waiting for transfers between devices: 58.1 us -> 74.2 us  [per_device(): lax.psum_scatter(contract_cols(branch_near, w_down), 'wide', scatter_dime...]
    unnamed x139 -> x135, local copies, waits for them, and re-layouts: 30.6 us -> 30.6 us
  transfers between devices with their start and end apart: 13 -> 15, of which waited for: 12 -> 12; matrix products, arithmetic and copies ran while one was open for 8% -> 9% of each run, Pallas kernels for 0% -> 0%
where the time goes in v1:
time: 1100 us
  waiting for transfers between devices  813 us (74%)
  matrix products  77.1 us (7%)
  blocking collectives  71.8 us (7%)
  local copies, waits for them, and re-layouts  68.7 us (6%)
  other arithmetic  38.2 us (3%)
  starting transfers between devices  17.1 us (2%)
  between operations  14.9 us (1%)
    psum x2, waiting for transfers between devices, per_device(): lax.psum((qkv_weight_grad, qkv_bias_grad, out_weight_grad, up_weight_grad...  423 us
    reduce_scatter x1, waiting for transfers between devices, per_device(): lax.psum_scatter(contract_cols(branch_near, w_down), 'wide', scatter_dime...  74.2 us
    reduce_scatter x1, waiting for transfers between devices, per_device(): lax.psum_scatter(up_part[None], 'wide', scatter_dimension=2, tiled=True)  72.4 us
    psum x1, waiting for transfers between devices, model_sum(): return lax.psum(parts, ('wide', 'narrow'))  68.4 us
    reduce_scatter x1, waiting for transfers between devices, per_device(): lax.psum_scatter(qkv_part, 'wide', scatter_dimension=2, tiled=True)  59.6 us
    psum x2, blocking collectives, model_sum(): return lax.psum(parts, ('wide', 'narrow'))  44 us
    unnamed x135, local copies, waits for them, and re-layouts  30.6 us
    reduce_scatter x1, waiting for transfers between devices, per_device(): lax.psum_scatter(contract_cols(branch_near, w_out), 'wide', scatter_dimen...  27 us
  transfers between devices with their start and end apart: 15, of which 12 were waited for; matrix products, arithmetic and copies ran while one was open for 9% of the time, Pallas kernels for 0%

profile of v1, /device:TPU:0, one launch (start us, length us, event | category | flops | bytes accessed | tf_op | source)
XLA Modules:
  0.0 1100.4 jit_solution(6887730244269682571)
XLA Ops:
  10.2 23.3 %all-reduce.2 = (f32[4,256]{1,0:T(4,128)S(1)}, f32[4,256]{1,0:T(4,128)S(1)}) all-reduce(f32[4,256]{1,0:T(4,128)S(1)} %get-tuple-element.142, f32[4,256]{1,0:T(4,128)S(1)} %get-tuple-element.141), channel_id=1, replica_groups=mesh['dp'=4,'wide'=4,'narrow'=2] {'wide','narrow'}, use_global_device_ids=true, to_apply=%region_3.0 | all-reduce | flops 2048 | bytes 16384 | tf_op jit(solution)/shard_map/psum | solution.py:38
  33.5 2.2 add_convert_fusion
  35.8 18.7 %all-gather.5.cloned.1.call-done = bf16[4,256,512]{2,1,0:T(8,128)(2,1)} async-done(((bf16[4,256,256]{2,1,0:T(8,128)(2,1)}), bf16[4,256,512]{2,1,0:T(8,128)(2,1)}) %all-gather.5.cloned.1.call-update) | async-done | bytes 1048592 | tf_op jit(solution)/shard_map/all_gather | solution.py:170
  54.4 5.6 convolution_bitcast_fusion
  60.1 3.8 fusion.72
  64.6 72.4 %reduce-scatter.9.cloned.1.call-done = f32[1,256,1024]{2,1,0:T(8,128)} async-done(((f32[1,256,4096]{2,1,0:T(8,128)}), f32[1,256,1024]{2,1,0:T(8,128)}) %reduce-scatter.9.cloned.1.call-update) | async-done | bytes 1048592 | tf_op jit(solution)/shard_map/reduce_scatter | solution.py:175
  136.9 2.2 multiply_convert_fusion
  141.1 59.6 %reduce-scatter.7.cloned.1.call-done = f32[3,256,256]{2,1,0:T(8,128)} async-done(((f32[3,256,1024]{2,1,0:T(8,128)}), f32[3,256,256]{2,1,0:T(8,128)}) %reduce-scatter.7.cloned.1.call-update) | async-done | bytes 786448 | tf_op jit(solution)/shard_map/reduce_scatter | solution.py:174
  214.0 22.1 %all_gather.16 = bf16[256,1024]{0,1:T(8,128)(2,1)} all-gather(bf16[256,256]{0,1:T(8,128)(2,1)S(1)} %bitcast.110), channel_id=1, replica_groups=mesh['dp'=4,'wide'=4,'narrow'=2] {'wide'}, dimensions={1}, use_global_device_ids=true | all-gather | bytes 655360 | tf_op jit(solution)/shard_map/all_gather | solution.py:193
  236.2 20.9 %all-gather.7.cloned.1.call-done = bf16[256,4096]{1,0:T(8,128)(2,1)} async-done(((bf16[256,1024]{1,0:T(8,128)(2,1)}), bf16[256,4096]{1,0:T(8,128)(2,1)}) %all-gather.7.cloned.1.call-update) | async-done | bytes 2097168 | tf_op jit(solution)/shard_map/all_gather | solution.py:194
  257.1 4.2 fusion.66
  262.6 2.1 convert_element_type.90
  265.9 3.7 fusion
  269.5 6.5 reduce-scatter.11.cloned.1.call-done
  277.9 2.6 convolution_bitcast_fusion.2
  281.7 1.9 copy.144
  288.1 68.4 %all-reduce.9.cloned.1.call-done = (f32[256,52]{0,1:T(8,128)}, f32[256]{0:T(256)}, f32[256,52]{0,1:T(8,128)}) async-done(((f32[256,52]{0,1:T(8,128)}, f32[256]{0:T(256)}, f32[256,52]{0,1:T(8,128)}), (f32[256,52]{0,1:T(8,128)}, f32[256]{0:T(256)}, f32[256,52]{0,1:T(8,128)})) %all-reduce.9.cloned.1.call-update) | async-done | bytes 107536 | tf_op jit(solution)/shard_map/psum | solution.py:38
  365.9 2.3 fusion.34
  368.2 2.4 convert_reduce_fusion.3
  370.6 5.6 all_gather.18
  376.3 5.5 fusion.69
  381.8 2.7 fusion.67
  384.6 74.2 %reduce-scatter.15.cloned.1.call-done = f32[256,1024]{1,0:T(8,128)} async-done(((f32[256,4096]{1,0:T(8,128)}), f32[256,1024]{1,0:T(8,128)}) %reduce-scatter.15.cloned.1.call-update) | async-done | bytes 1048592 | tf_op jit(solution)/shard_map/reduce_scatter | solution.py:251
  458.7 3.4 convert_reduce_fusion
  462.2 27.0 %reduce-scatter.13.cloned.1.call-done = f32[256,256]{1,0:T(8,128)} async-done(((f32[256,1024]{1,0:T(8,128)}), f32[256,256]{1,0:T(8,128)}) %reduce-scatter.13.cloned.1.call-update) | async-done | bytes 262160 | tf_op jit(solution)/shard_map/reduce_scatter | solution.py:248
  504.5 2.3 convert_reduce_fusion.1
  506.8 3.8 collective-permute-start.1
  510.6 18.7 %collective-permute-done = bf16[3,256,256]{1,2,0:T(8,128)(2,1)} collective-permute-done((bf16[3,256,256]{1,2,0:T(8,128)(2,1)}, bf16[3,256,256]{1,2,0:T(8,128)(2,1)}, u32[]{:S(2)}, u32[]{:S(2)}) %collective-permute-start) | collective-permute-done | bytes 393248 | tf_op jit(solution)/shard_map/ppermute | solution.py:25
  529.3 12.4 %collective-permute-start.2 = (bf16[3,256,256]{1,2,0:T(8,128)(2,1)}, bf16[3,256,256]{1,2,0:T(8,128)(2,1)}, u32[]{:S(2)}, u32[]{:S(2)}) collective-permute-start(bf16[3,256,256]{1,2,0:T(8,128)(2,1)} %collective-permute-done), channel_id=1, source_target_pairs={{0,2},{2,4},{4,6},{6,0},{1,3},{3,5},{5,7},{7,1},{8,10},{10,12},{12... | collective-permute-start | bytes 1179656 | tf_op jit(solution)/shard_map/ppermute | solution.py:25
  541.7 1.9 copy.157
  546.7 1.9 copy.158
  548.6 1.9 copy.159
  554.1 7.5 collective-permute-done.2
  561.6 1.9 copy.160
  565.3 3.6 fusion.68
  568.9 4.2 convolution_bitcast_fusion.1
  579.6 4.7 fusion.71
  584.3 5.4 fusion.73
  589.7 15.1 %reduce-scatter.17.cloned.1.call-done = f32[4,256,256]{2,1,0:T(8,128)} async-done(((f32[4,256,512]{2,1,0:T(8,128)}), f32[4,256,256]{2,1,0:T(8,128)}) %reduce-scatter.17.cloned.1.call-update) | async-done | bytes 1048592 | tf_op jit(solution)/shard_map/reduce_scatter | solution.py:284
  604.8 2.6 multiply_reduce_fusion
  607.5 5.6 fusion.31
  615.0 3.3 convert_bitcast_fusion
  620.1 3.7 fusion.10
  624.6 20.7 %all-reduce = (f32[4,256]{1,0:T(4,128)S(1)}, f32[4,256]{1,0:T(4,128)S(1)}) all-reduce(f32[4,256]{1,0:T(4,128)S(1)} %get-tuple-element.138, f32[4,256]{1,0:T(4,128)S(1)} %get-tuple-element.139), channel_id=1, replica_groups=mesh['dp'=4,'wide'=4,'narrow'=2] {'wide','narrow'}, use_global_device_ids=true, to_apply=%region_21.22 | all-reduce | flops 2048 | bytes 16384 | tf_op jit(solution)/shard_map/psum | solution.py:38
  647.0 423.5 %all-reduce.13.cloned.1.call-done = (f32[3,512,1024]{2,1,0:T(8,128)}, f32[1024,512]{1,0:T(8,128)}, f32[512,4096]{1,0:T(8,128)}, f32[4096,512]{1,0:T(8,128)}) async-done(((f32[3,512,1024]{2,1,0:T(8,128)}, f32[1024,512]{1,0:T(8,128)}, f32[512,4096]{1,0:T(8,128)}, f32[4096,512]{1,0:T(8,128)}), (f32[3,512,1024]{2,1,0:T(8,128)}, f32[1024,512]{1,0:T(8,128)}, f32[512,4096]{1,0:T(8,128)}, ...) | async-done | bytes 25165840 | tf_op jit(solution)/shard_map/psum | solution.py:296
  1070.5 7.1 copy.251
  1079.5 4.3 copy.254
  1085.5 3.9 copy.256
  (229 shorter events, 82.4 us)
Async XLA Ops:
  7.2 52.9 %copy-start = (bf16[3,512,1024]{2,1,0:T(8,128)(2,1)S(1)}, bf16[3,512,1024]{2,1,0:T(8,128)(2,1)}, u32[]{:S(2)}) copy-start(bf16[3,512,1024]{2,1,0:T(8,128)(2,1)} %param.21) | copy-start | bytes 9437188
  7.2 47.2 %all-gather.5.cloned.1.call-start = ((), (), s32[]{:S(2)}) async-start(), calls=%async_computation.6 | async-start | bytes 1572864 | tf_op jit(solution)/shard_map/all_gather | solution.py:170
  35.7 101.2 %reduce-scatter.9.cloned.1.call-start = ((), (), s32[]{:S(2)}) async-start(), calls=%async_computation.8 | async-start | bytes 5242880 | tf_op jit(solution)/shard_map/reduce_scatter | solution.py:175
  60.0 140.7 %reduce-scatter.7.cloned.1.call-start = ((), (), s32[]{:S(2)}) async-start(), calls=%async_computation.7 | async-start | bytes 3932160 | tf_op jit(solution)/shard_map/reduce_scatter | solution.py:174
  63.9 75.4 %copy-start.50 = (bf16[3,256]{1,0:T(4,128)(2,1)S(1)}, bf16[3,256]{1,0:T(4,128)(2,1)}, u32[]{:S(2)}) copy-start(bf16[3,256]{1,0:T(4,128)(2,1)} %param.22) | copy-start | bytes 4612
  63.9 193.2 %all-gather.7.cloned.1.call-start = ((), (), s32[]{:S(2)}) async-start(), calls=%async_computation.9 | async-start | bytes 2621440 | tf_op jit(solution)/shard_map/all_gather | solution.py:194
  64.6 138.0 %copy-start.39 = (f32[1024]{0:T(1024)}, f32[1024]{0:T(1024)S(1)}, u32[]{:S(2)}) copy-start(f32[1024]{0:T(1024)S(1)} %convert_element_type.100) | copy-start | bytes 12292
  139.2 136.9 %reduce-scatter.11.cloned.1.call-start = ((), (), s32[]{:S(2)}) async-start(), calls=%async_computation.10 | async-start | bytes 786432 | tf_op jit(solution)/shard_map/reduce_scatter | solution.py:200
  257.1 4.2 copy-start.6
  257.1 4.2 copy-start.11
  261.3 3.5 copy-start.53
  261.3 4.0 copy-start.54
  262.6 93.8 %all-reduce.9.cloned.1.call-start = ((), (), s32[]{:S(2)}) async-start(), calls=%async_computation.15 | async-start | bytes 231424 | tf_op jit(solution)/shard_map/psum | solution.py:38
  276.1 4.4 copy-start.31
  277.9 90.3 %copy-start.9 = (f32[256,256]{1,0:T(8,128)}, f32[256,256]{1,0:T(8,128)S(1)}, u32[]{:S(2)}) copy-start(f32[256,256]{1,0:T(8,128)S(1)} %get-tuple-element.171) | copy-start | bytes 786436
  286.7 172.1 %reduce-scatter.15.cloned.1.call-start = ((), (), s32[]{:S(2)}) async-start(), calls=%async_computation.12 | async-start | bytes 5242880 | tf_op jit(solution)/shard_map/reduce_scatter | solution.py:251
  381.8 107.5 %reduce-scatter.13.cloned.1.call-start = ((), (), s32[]{:S(2)}) async-start(), calls=%async_computation.11 | async-start | bytes 1310720 | tf_op jit(solution)/shard_map/reduce_scatter | solution.py:248
  384.5 184.3 %all-gather.9.cloned.1.call-start = ((), (), s32[]{:S(2)}) async-start(), calls=%async_computation.14 | async-start | bytes 2621440 | tf_op jit(solution)/shard_map/all_gather | solution.py:271
  462.2 142.6 %reduce-scatter.17.cloned.1.call-start = ((), (), s32[]{:S(2)}) async-start(), calls=%async_computation.13 | async-start | bytes 3145728 | tf_op jit(solution)/shard_map/reduce_scatter | solution.py:284
  492.6 3.2 copy-start.16
  492.6 3.2 copy-start.18
  492.6 3.2 copy-start.25
  506.8 22.5 %collective-permute-start = (bf16[3,256,256]{1,2,0:T(8,128)(2,1)}, bf16[3,256,256]{1,2,0:T(8,128)(2,1)}, u32[]{:S(2)}, u32[]{:S(2)}) collective-permute-start(bf16[3,256,256]{1,2,0:T(8,128)(2,1)} %get-tuple-element.169), channel_id=1, source_target_pairs={{0,2},{2,4},{4,6},{6,0},{1,3},{3,5},{5,7},{7,1},{8,10},{10,12},{12... | collective-permute-start | bytes 1179656 | tf_op jit(solution)/shard_map/ppermute | solution.py:25
  506.8 41.8 %collective-permute-start.1 = (bf16[3,256,256]{1,2,0:T(8,128)(2,1)}, bf16[3,256,256]{1,2,0:T(8,128)(2,1)}, u32[]{:S(2)}, u32[]{:S(2)}) collective-permute-start(bf16[3,256,256]{1,2,0:T(8,128)(2,1)} %get-tuple-element.169), channel_id=1, source_target_pairs={{0,6},{2,0},{4,2},{6,4},{1,7},{3,1},{5,3},{7,5},{8,14},{10,8},{12,... | collective-permute-start | bytes 1179656 | tf_op jit(solution)/shard_map/ppermute | solution.py:30
  529.3 32.3 %collective-permute-start.2 = (bf16[3,256,256]{1,2,0:T(8,128)(2,1)}, bf16[3,256,256]{1,2,0:T(8,128)(2,1)}, u32[]{:S(2)}, u32[]{:S(2)}) collective-permute-start(bf16[3,256,256]{1,2,0:T(8,128)(2,1)} %collective-permute-done), channel_id=1, source_target_pairs={{0,2},{2,4},{4,6},{6,0},{1,3},{3,5},{5,7},{7,1},{8,10},{10,12},{12... | collective-permute-start | bytes 1179656 | tf_op jit(solution)/shard_map/ppermute | solution.py:25
  568.9 4.2 copy-start.5
  574.7 5.0 copy-start.12
  574.7 72.4 %all-reduce.11.cloned.1.call-start = ((), (), s32[]{:S(2)}) async-start(), calls=%async_computation.16 | async-start | bytes 209920 | tf_op jit(solution)/shard_map/psum | solution.py:296
  579.6 4.7 copy-start.32
  584.3 20.4 %copy-start.3 = (bf16[4,256,256]{2,1,0:T(8,128)(2,1)S(1)}, bf16[4,256,256]{2,1,0:T(8,128)(2,1)}, u32[]{:S(2)}) copy-start(bf16[4,256,256]{2,1,0:T(8,128)(2,1)} %param.18) | copy-start | bytes 1572868
  584.3 23.2 %copy-start.14 = (bf16[256,4096]{1,0:T(8,128)(2,1)S(1)}, bf16[256,4096]{1,0:T(8,128)(2,1)}, u32[]{:S(2)}) copy-start(bf16[256,4096]{1,0:T(8,128)(2,1)} %all-gather.9.cloned.1.call-done) | copy-start | bytes 6291460
  607.4 463.1 %all-reduce.13.cloned.1.call-start = ((), (), s32[]{:S(2)}) async-start(), calls=%async_computation.17 | async-start | bytes 50331648 | tf_op jit(solution)/shard_map/psum | solution.py:296
  620.1 25.3 %copy-start.8 = (f32[4,256,256]{2,1,0:T(8,128)S(1)}, f32[4,256,256]{2,1,0:T(8,128)}, u32[]{:S(2)}) copy-start(f32[4,256,256]{2,1,0:T(8,128)} %reduce-scatter.17.cloned.1.call-done) | copy-start | bytes 3145732
  623.8 22.3 %copy-start.28 = (f32[256,256]{1,0:T(8,128)S(1)}, f32[256,256]{1,0:T(8,128)}, u32[]{:S(2)}) copy-start(f32[256,256]{1,0:T(8,128)} %get-tuple-element.165) | copy-start | bytes 786436
  1070.5 7.1 copy-start.48
  1070.5 7.7 copy-start.13
  1070.5 9.0 copy-start.4
  1078.2 6.2 slice-start
  1079.5 4.3 copy-start.47
  1079.5 6.0 slice-start.1
  1085.5 4.0 copy-start.52
  1085.5 4.5 copy-start.46
  1085.5 5.1 copy-start.45
  1085.5 5.7 copy-start.51
  1085.5 6.3 copy-start.38
  1085.5 6.9 copy-start.41
  1085.5 7.5 copy-start.55
  1085.5 8.0 copy-start.1
  (25 other events, 45.7 us)
Sparse Core Ops, SparseCore 0:
  35.8 18.5 all-gather.4
  60.1 76.7 reduce-scatter.8
  139.9 60.7 reduce-scatter.6
  202.8 54.2 all-gather.6
  262.7 13.3 reduce-scatter.10
  286.8 69.6 all-reduce.8
  381.9 76.7 reduce-scatter.14
  461.6 27.6 reduce-scatter.12
  491.5 67.5 all-gather.8
  574.8 29.9 reduce-scatter.16
  608.9 30.8 all-reduce.10
  643.8 426.6 all-reduce.12
